TPU v7x, 32 devices: a whole 2x2x4 slice. The times are simulated.
32 devices in a mesh: seq: 8 (over z, y), exp: 4 (over x, core).
Axes of the slice: x: 2, y: 2, z: 4, core: 2. Of those that a mesh axis runs over, the one named last changes fastest.
Arguments:
- queries: bfloat16 [2048, 6144], P('seq', 'exp'), may hold values from -6 to 6
- key_rows: bfloat16 [2048, 6144], P('seq', 'exp'), may hold values from -6 to 6
- value_rows: bfloat16 [2048, 6144], P('seq', 'exp'), may hold values from -6 to 6
- log_decay: float32 [2048, 48], P('seq', 'exp'), may hold values from -1 to 0, as said below
- residual: bfloat16 [2048, 6144], P('seq', 'exp'), may hold values from -6 to 6
- head_gain: float32 [6144], P('exp'), may hold values from 0.1 to 1.9
- moe_gain: float32 [6144], replicated, may hold values from 0.1 to 1.9
- routes: int32 [2048, 2], P(('seq', 'exp')), may hold values from 0 to 7, all different within a row; in each aligned block of 64 rows (0 to 63, 64 to 127, ...) at most 20 rows name the same one
- route_weight: float32 [2048, 2], P(('seq', 'exp')), may hold values from 0.2 to 1
- up_weight: bfloat16 [8, 6144, 9216], P('exp', None, 'seq'), may hold values from -0.078125 to 0.078125
- down_weight: bfloat16 [8, 9216, 6144], P('exp', 'seq'), may hold values from -0.0625 to 0.0625
Outputs:
- layer_out: bfloat16 [2048, 6144], P(('seq', 'exp'))
Inputs may be any that keep to these rules, and one draw needn't show every extreme that they name: `log_decay`: every entry is negative. `routes`: A row names two different experts. In each aligned block of 64 rows no expert is named more than 20 times, a bound that some block reaches.
All inputs are finite; a program needn't handle non-finite values.
Results may differ from a plain program's by a relative error of at most 0.012.
Values may be sent and summed in bfloat16 or wider, within the bound.
A program may use at most 192 MiB of HBM per device.

v0:
```python
import jax
import jax.numpy as jnp
from jax import lax
from jax.sharding import PartitionSpec as P

HEAD_DIM = 128
BLK = 256
EXPERTS = 8


def expert_part(received, up_weight, down_weight):
    hidden = jax.nn.silu(
        jnp.einsum("sxkd,xdh->sxkh", received, up_weight, preferred_element_type=jnp.float32)
    ).astype(jnp.bfloat16)
    return jnp.einsum(
        "sxkh,xhd->sxkd", hidden, down_weight, preferred_element_type=jnp.float32
    ).astype(jnp.bfloat16)


def per_device(
    queries,
    key_rows,
    value_rows,
    log_decay,
    residual,
    head_gain,
    moe_gain,
    routes,
    route_weight,
    up_weight,
    down_weight,
):
    token_count, feature_dim = queries.shape
    head_count = log_decay.shape[1]
    block_count = token_count // BLK
    shaped = (block_count, BLK, head_count, HEAD_DIM)
    query_blk = queries.reshape(shaped)
    key_blk = key_rows.reshape(shaped)
    value_blk = value_rows.reshape(shaped)
    cumulative = jnp.cumsum(log_decay.reshape(block_count, BLK, head_count), axis=1)
    totals = cumulative[:, -1, :]
    scores = jnp.einsum("bthd,bjhd->bhtj", query_blk, key_blk, preferred_element_type=jnp.float32)
    levels = jnp.transpose(cumulative, (0, 2, 1))
    spread = levels[:, :, :, None] - levels[:, :, None, :]
    causal = jnp.tril(jnp.ones((BLK, BLK), dtype=bool))[None, None]
    weights = (jnp.where(causal, jnp.exp(jnp.where(causal, spread, 0.0)), 0.0) * scores).astype(
        jnp.bfloat16
    )
    inner_part = jnp.einsum(
        "bhtj,bjhd->bthd", weights, value_blk, preferred_element_type=jnp.float32
    )
    fading = jnp.exp(totals[:, None, :] - cumulative)
    key_faded = (fading[..., None] * key_blk.astype(jnp.float32)).astype(jnp.bfloat16)
    block_states = jnp.einsum(
        "bjhd,bjhe->bhde", key_faded, value_blk, preferred_element_type=jnp.float32
    )

    def advance(running, pair_item):
        total_row, state_row = pair_item
        return (jnp.exp(total_row)[:, None, None] * running + state_row, running)

    empty_state = jnp.zeros((head_count, HEAD_DIM, HEAD_DIM), jnp.float32)
    own_state, local_prev = lax.scan(advance, empty_state, (totals, block_states))
    own_log = jnp.sum(totals, axis=0)
    logs_all, states_all = (
        lax.all_gather(own_log[None].astype(jnp.bfloat16), "seq", axis=0, tiled=True).astype(
            jnp.float32
        ),
        lax.all_gather(own_state[None].astype(jnp.bfloat16), "seq", axis=0, tiled=True).astype(
            jnp.float32
        ),
    )
    position = lax.axis_index("seq")
    below_me = jnp.arange(logs_all.shape[0])[:, None] < position
    inclusive = jnp.cumsum(logs_all, axis=0)
    before = jnp.sum(jnp.where(below_me, logs_all, 0.0), axis=0)
    factors = jnp.where(
        below_me, jnp.exp(jnp.where(below_me, before[None, :] - inclusive, 0.0)), 0.0
    )
    incoming = jnp.einsum("sh,shde->hde", factors, states_all, precision=lax.Precision.HIGHEST)
    starts = jnp.concatenate(
        [jnp.zeros((1, head_count), jnp.float32), jnp.cumsum(totals, axis=0)[:-1]], axis=0
    )
    carried = jnp.exp(starts)[:, :, None, None] * incoming[None] + local_prev
    query_faded = jnp.exp(cumulative)[..., None] * query_blk.astype(jnp.float32)
    carried_part = jnp.einsum(
        "bthd,bhde->bthe", query_faded, carried, precision=lax.Precision.HIGHEST
    )
    attention = carried_part + inner_part
    mean_square = jnp.mean(attention * attention, axis=-1, keepdims=True)
    normed = attention * lax.rsqrt(mean_square + 1e-06) * head_gain.reshape(head_count, HEAD_DIM)
    mixed_rows = (residual.astype(jnp.float32) + normed.reshape(token_count, feature_dim)).astype(
        jnp.bfloat16
    )
    token_rows = lax.all_to_all(mixed_rows, "exp", split_axis=0, concat_axis=1, tiled=True)
    row_count, model_dim = token_rows.shape
    token_float = token_rows.astype(jnp.float32)
    row_square = jnp.mean(token_float * token_float, axis=-1, keepdims=True)
    norm_rows = (token_float * lax.rsqrt(row_square + 1e-06) * moe_gain).astype(jnp.bfloat16)
    capacity = row_count * 10 // (4 * EXPERTS)
    flat_ids = routes.reshape(-1)
    onehot = (flat_ids[:, None] == jnp.arange(EXPERTS, dtype=jnp.int32)[None, :]).astype(jnp.int32)
    slot_rank = jnp.sum((jnp.cumsum(onehot, axis=0) - 1) * onehot, axis=1)
    slot_index = flat_ids * capacity + slot_rank
    placer = jnp.arange(EXPERTS * capacity, dtype=jnp.int32)[:, None] == slot_index[None, :]
    placer = jnp.any(placer.reshape(EXPERTS * capacity, row_count, 2), axis=2).astype(jnp.bfloat16)
    packed = jnp.dot(placer, norm_rows, preferred_element_type=jnp.float32).astype(jnp.bfloat16)
    seq_count = lax.axis_size("seq")
    exp_count = lax.axis_size("exp")
    local_experts = up_weight.shape[0]
    buffer = jnp.broadcast_to(
        packed.reshape(1, exp_count, local_experts, capacity, model_dim),
        (seq_count, exp_count, local_experts, capacity, model_dim),
    )
    buffer = buffer.reshape(seq_count * exp_count, local_experts, capacity, model_dim)
    answered = expert_part(
        lax.all_to_all(buffer, ("seq", "exp"), split_axis=0, concat_axis=0, tiled=True),
        up_weight,
        down_weight,
    )
    returned = lax.all_to_all(answered, ("seq", "exp"), split_axis=0, concat_axis=0, tiled=True)
    summed = jnp.sum(
        returned.reshape(seq_count, EXPERTS * capacity, model_dim), axis=0, dtype=jnp.float32
    )
    picked = jnp.take(summed, slot_index, axis=0).reshape(row_count, 2, model_dim)
    combined = jnp.sum(picked * route_weight[:, :, None], axis=1)
    return (token_float + combined).astype(jnp.bfloat16)


def solution(mesh):
    return jax.shard_map(
        per_device,
        mesh=mesh,
        in_specs=(
            P("seq", "exp"),
            P("seq", "exp"),
            P("seq", "exp"),
            P("seq", "exp"),
            P("seq", "exp"),
            P("exp"),
            P(),
            P(("seq", "exp"), None),
            P(("seq", "exp"), None),
            P("exp", None, "seq"),
            P("exp", "seq", None),
        ),
        out_specs=P(("seq", "exp"), None),
        check_vma=False,
    )
```

profile of v0, /device:TPU:0, one launch (start us, length us, event | category | flops | bytes accessed | tf_op | source)
XLA Modules:
  0.0 1033.3 jit_solution(2493451513064124806)
XLA Ops:
  6.5 0.8 reshape.270
  7.3 0.6 reduce-window.6
  7.9 0.2 slice_reduce_fusion
  8.1 0.1 copy.151
  8.3 0.0 copy-start.3
  8.4 0.1 copy.153
  8.4 1.5 copy.154
  9.9 0.0 copy-start.6
  10.0 0.3 copy.155
  10.2 0.0 copy-start.4
  10.2 1.1 fusion.19
  11.4 0.0 all-gather.4.cloned.1.call-update
  11.4 22.2 %all-gather = bf16[8,1,12]{2,1,0:T(2,128)(2,1)S(1)} all-gather(bf16[1,1,12]{2,1,0:T(2,128)(2,1)S(1)} %slice.22), channel_id=2, replica_groups=mesh['seq'=8,'exp'=4] {'seq'}, dimensions={0}, use_global_device_ids=true | all-gather | bytes 216 | tf_op jit(solution)/shard_map/all_gather | solution.py:66
  33.6 0.1 copy.157
  33.7 0.3 copy.158
  34.0 0.1 copy.193
  34.1 0.1 copy.166
  34.2 0.1 reshape.281
  34.4 0.1 select_reduce_fusion.1
  34.5 0.1 select_bitcast_fusion
  34.6 40.1 %all-gather.4.cloned.1.call-done = bf16[96,128,128]{2,1,0:T(8,128)(2,1)} async-done(((bf16[12,128,128]{2,1,0:T(8,128)(2,1)}), bf16[96,128,128]{2,1,0:T(8,128)(2,1)}) %all-gather.4.cloned.1.call-update) | async-done | bytes 3145744 | tf_op jit(solution)/shard_map/all_gather | solution.py:69
  74.7 2.6 multiply_reduce_fusion
  77.4 1.6 fusion.16
  79.0 0.0 copy-start.8
  79.0 3.8 fusion.14
  82.8 1.7 fusion.15
  84.5 0.5 copy.164
  85.0 2.2 add_convert_fusion.1
  87.2 3.5 all-to-all-start
  90.7 0.1 fusion.25
  90.8 0.2 reduce_window_sum.59
  90.9 0.2 select_reduce_fusion
  91.1 0.1 reduce_sum.65
  91.3 0.1 copy.167
  91.3 0.6 compare_and_fusion
  91.9 0.1 fusion.24
  92.0 10.3 all-to-all-done
  102.3 0.2 convert_bitcast_fusion.1
  102.5 0.1 copy.196
  102.6 0.3 fusion.13
  102.9 0.9 copy-done
  103.7 2.0 convolution_convert_fusion
  105.8 2.5 broadcast_in_dim.90
  108.3 2.0 copy.169
  110.3 12.7 %broadcast_in_dim.91 = bf16[8,4,2,20,6144]{4,2,3,1,0:T(2,128)(2,1)S(1)} broadcast(bf16[4,2,20,6144]{3,1,2,0:T(2,128)(2,1)S(1)} %copy.169), dimensions={1,2,3,4} | broadcast | bytes 17694720 | tf_op jit(solution)/shard_map/broadcast_in_dim | solution.py:111
  123.0 343.5 %all_to_all.23 = bf16[32,2,20,6144]{3,1,2,0:T(2,128)(2,1)S(1)} all-to-all(bf16[32,2,20,6144]{3,1,2,0:T(2,128)(2,1)S(1)} %bitcast.100), channel_id=1, replica_groups=mesh['seq'=8,'exp'=4] {'seq','exp'}, dimensions={0} | all-to-all | bytes 31457280 | tf_op jit(solution)/shard_map/all_to_all | solution.py:117
  466.5 48.6 %fusion.2 = f32[2,32,20,1152]{3,1,2,0:T(8,128)} fusion(bf16[2,6144,1152]{2,1,0:T(8,128)(2,1)} %param.20, bf16[32,2,20,6144]{3,1,2,0:T(2,128)(2,1)S(1)} %all_to_all.23), kind=kOutput, calls=%fused_computation.3 | convolution fusion | flops 18119393280 | bytes 49938432 | tf_op jit(solution)/shard_map/sxkd,xdh->sxkh/dot_general | solution.py:13
  515.0 28.8 %convert_bitcast_fusion = bf16[32,2,20,6144]{3,0,2,1:T(8,128)(2,1)} fusion(bf16[2,1152,6144]{2,1,0:T(8,128)(2,1)} %param.21, f32[2,32,20,1152]{3,1,2,0:T(8,128)} %fusion.2), kind=kOutput, calls=%fused_computation.7 | convolution fusion | flops 18134630400 | bytes 49938432 | tf_op jit(solution)/shard_map/sxkh,xhd->sxkd/dot_general | solution.py:15
  543.8 29.6 %copy.172 = bf16[32,2,20,6144]{3,1,2,0:T(2,128)(2,1)} copy(bf16[32,2,20,6144]{3,0,2,1:T(8,128)(2,1)} %convert_bitcast_fusion) | data formatting | bytes 31457280 | tf_op jit(solution)/shard_map/convert_element_type | solution.py:17
  573.4 0.0 copy-start.12
  573.4 4.5 all-to-all-start.2
  578.0 0.1 copy.175
  578.1 0.1 mul.147
  578.2 0.1 copy.168
  578.4 0.1 copy.176
  578.5 348.8 %all-to-all-done.2 = bf16[32,2,20,6144]{3,1,2,0:T(2,128)(2,1)} async-done(((bf16[32,2,20,6144]{3,1,2,0:T(2,128)(2,1)}), bf16[32,2,20,6144]{3,1,2,0:T(2,128)(2,1)}, u32[]{:S(2)}, u32[]{:S(2)}) %all-to-all-start.2) | async-done | bytes 15728672 | tf_op jit(solution)/shard_map/all_to_all | solution.py:121
  927.2 9.5 copy_convert_fusion
  936.8 24.0 %copy.174 = f32[32,2,20,6144]{3,2,1,0:T(8,128)} copy(f32[32,2,20,6144]{3,0,2,1:T(8,128)S(1)} %copy_convert_fusion) | data formatting | bytes 62914560 | tf_op jit(solution)/shard_map/convert_element_type | solution.py:122
  960.8 34.9 %reshape.284 = f32[8,160,6144]{2,1,0:T(8,128)} reshape(f32[32,2,20,6144]{3,2,1,0:T(8,128)} %copy.174) | data formatting | bytes 62914560 | tf_op jit(solution)/shard_map/convert_element_type | solution.py:122
  995.7 13.4 %reduce_sum.67 = f32[160,6144]{1,0:T(8,128)} reduce(f32[8,160,6144]{2,1,0:T(8,128)} %reshape.284, f32[]{:T(128)} %constant.38.clone.1), dimensions={0}, to_apply=%region_9.10 | reduce | flops 6881280 | bytes 35389444 | tf_op jit(solution)/shard_map/reduce_sum | solution.py:122
  1009.2 6.6 gather_fusion
  1015.8 3.9 gather.7
  1019.7 5.4 multiply_reduce_fusion.1
  1025.1 1.0 add_convert_fusion
  (44 shorter events, 0.3 us)
Async XLA Ops:
  6.5 3.4 copy-start.2
  6.5 68.2 %all-gather.4.cloned.1.call-start = ((), (), s32[]{:S(2)}) async-start(), calls=%async_computation.3 | async-start | bytes 3538944 | tf_op jit(solution)/shard_map/all_gather | solution.py:69
  8.3 25.4 %copy-start.3 = (bf16[256,1536]{1,0:T(8,128)(2,1)S(1)}, bf16[256,1536]{1,0:T(8,128)(2,1)}, u32[]{:S(2)}) copy-start(bf16[256,1536]{1,0:T(8,128)(2,1)} %param.11) | copy-start | bytes 2359300
  9.9 24.2 %copy-start.6 = (s32[64,2]{0,1:T(2,128)S(1)}, s32[64,2]{0,1:T(2,128)}, u32[]{:S(2)}) copy-start(s32[64,2]{0,1:T(2,128)} %param.18) | copy-start | bytes 1540
  10.2 67.1 %copy-start.4 = (bf16[256,1536]{0,1:T(8,128)(2,1)}, bf16[256,1536]{0,1:T(8,128)(2,1)S(1)}, u32[]{:S(2)}) copy-start(bf16[256,1536]{0,1:T(8,128)(2,1)S(1)} %copy.155) | copy-start | bytes 2359300
  79.0 3.8 copy-start.8
  87.2 15.1 %all-to-all-start = ((bf16[4,64,1536]{2,1,0:T(8,128)(2,1)}), bf16[4,64,1536]{2,1,0:T(8,128)(2,1)S(1)}, u32[]{:S(2)}, u32[]{:S(2)}) async-start(bf16[4,64,1536]{2,1,0:T(8,128)(2,1)} %bitcast.25), calls=%async_computation | async-start | bytes 1572864 | tf_op jit(solution)/shard_map/all_to_all | solution.py:95
  91.1 11.8 %copy-start.9 = (s32[128]{0:T(128)}, s32[128]{0:T(128)S(1)}, u32[]{:S(2)}) copy-start(s32[128]{0:T(128)S(1)} %select_reduce_fusion) | copy-start | bytes 1540
  92.0 11.7 %copy-start.5 = (f32[6144]{0:T(1024)S(1)}, f32[6144]{0:T(1024)}, u32[]{:S(2)}) copy-start(f32[6144]{0:T(1024)} %param.17) | copy-start | bytes 73732
  102.6 1.1 copy-start
  573.4 4.6 copy-start.7
  573.4 4.8 copy-start.11
  573.4 4.9 copy-start.12
  573.4 5.0 copy-start.10
  573.4 353.8 %all-to-all-start.2 = ((bf16[32,2,20,6144]{3,1,2,0:T(2,128)(2,1)}), bf16[32,2,20,6144]{3,1,2,0:T(2,128)(2,1)}, u32[]{:S(2)}, u32[]{:S(2)}) async-start(bf16[32,2,20,6144]{3,1,2,0:T(2,128)(2,1)} %copy.172), calls=%async_computation.2 | async-start | bytes 31457280 | tf_op jit(solution)/shard_map/all_to_all | solution.py:121
  1019.7 5.4 copy-start.1
Sparse Core Ops, SparseCore 0:
  11.5 63.1 all-gather.3
where the time goes:
time: 1040 us; the launch traced here: 1030 us
  waiting for transfers between devices  399 us (38%)
  blocking collectives  366 us (35%)
  local copies, waits for them, and re-layouts  122 us (12%)
  matrix products  85.9 us (8%)
  other arithmetic  38.4 us (4%)
  between operations  14.1 us (1%)
    all_to_all x1, waiting for transfers between devices, per_device(): lax.all_to_all(answered, ('seq', 'exp'), split_axis=0, concat_axis=0, til...  349 us
    all_to_all x1, blocking collectives, per_device(): lax.all_to_all(buffer, ('seq', 'exp'), split_axis=0, concat_axis=0, tiled...  343 us
    convert_element_type x2, local copies, waits for them, and re-layouts, per_device(): jnp.sum(returned.reshape(seq_count, EXPERTS * capacity, model_dim), axis=...  58.9 us
    dot_general x1, matrix products, expert_part(): jnp.einsum('sxkd,xdh->sxkh', received, up_weight, preferred_element_type=...  48.6 us
    all_gather x1, waiting for transfers between devices, per_device(): lax.all_gather(own_state[None].astype(jnp.bfloat16), 'seq', axis=0, tiled...  40.1 us
    convert_element_type x1, local copies, waits for them, and re-layouts, expert_part(): return jnp.einsum('sxkh,xhd->sxkd', hidden, down_weight, preferred_elemen...  29.6 us
    dot_general x1, matrix products, expert_part(): jnp.einsum('sxkh,xhd->sxkd', hidden, down_weight, preferred_element_type=...  28.8 us
    all_gather x1, blocking collectives, per_device(): lax.all_gather(own_log[None].astype(jnp.bfloat16), 'seq', axis=0, tiled=T...  22.2 us
  transfers between devices with their start and end apart: 3, of which 3 were waited for; matrix products, arithmetic and copies ran while one was open for 0% of the time, Pallas kernels for 0%

commit v1 on v0

--- a/solution.py
+++ b/solution.py
@@ -8,13 +8,11 @@
 EXPERTS = 8
 
 
-def expert_part(received, up_weight, down_weight):
-    hidden = jax.nn.silu(
-        jnp.einsum("sxkd,xdh->sxkh", received, up_weight, preferred_element_type=jnp.float32)
-    ).astype(jnp.bfloat16)
-    return jnp.einsum(
-        "sxkh,xhd->sxkd", hidden, down_weight, preferred_element_type=jnp.float32
-    ).astype(jnp.bfloat16)
+def expert_part(rows, up_weight, down_weight):
+    hidden = jax.nn.silu(jnp.dot(rows, up_weight, preferred_element_type=jnp.float32)).astype(
+        jnp.bfloat16
+    )
+    return jnp.dot(hidden, down_weight, preferred_element_type=jnp.float32).astype(jnp.bfloat16)
 
 
 def per_device(
@@ -62,14 +60,12 @@
     empty_state = jnp.zeros((head_count, HEAD_DIM, HEAD_DIM), jnp.float32)
     own_state, local_prev = lax.scan(advance, empty_state, (totals, block_states))
     own_log = jnp.sum(totals, axis=0)
-    logs_all, states_all = (
-        lax.all_gather(own_log[None].astype(jnp.bfloat16), "seq", axis=0, tiled=True).astype(
-            jnp.float32
-        ),
-        lax.all_gather(own_state[None].astype(jnp.bfloat16), "seq", axis=0, tiled=True).astype(
-            jnp.float32
-        ),
-    )
+    log_plane = jnp.zeros((1, HEAD_DIM, HEAD_DIM), jnp.bfloat16)
+    log_plane = log_plane.at[0, 0, :head_count].set(own_log.astype(jnp.bfloat16))
+    payload = jnp.concatenate([own_state.astype(jnp.bfloat16), log_plane], axis=0)
+    gathered = lax.all_gather(payload, "seq", axis=0, tiled=False).astype(jnp.float32)
+    states_all = gathered[:, :head_count]
+    logs_all = gathered[:, head_count, 0, :head_count]
     position = lax.axis_index("seq")
     below_me = jnp.arange(logs_all.shape[0])[:, None] < position
     inclusive = jnp.cumsum(logs_all, axis=0)
@@ -103,27 +99,26 @@
     slot_rank = jnp.sum((jnp.cumsum(onehot, axis=0) - 1) * onehot, axis=1)
     slot_index = flat_ids * capacity + slot_rank
     placer = jnp.arange(EXPERTS * capacity, dtype=jnp.int32)[:, None] == slot_index[None, :]
-    placer = jnp.any(placer.reshape(EXPERTS * capacity, row_count, 2), axis=2).astype(jnp.bfloat16)
-    packed = jnp.dot(placer, norm_rows, preferred_element_type=jnp.float32).astype(jnp.bfloat16)
-    seq_count = lax.axis_size("seq")
+    placed = placer.reshape(EXPERTS * capacity, row_count, 2)
+    packer = jnp.any(placed, axis=2).astype(jnp.bfloat16)
+    packed = jnp.dot(packer, norm_rows, preferred_element_type=jnp.float32).astype(jnp.bfloat16)
+    combiner = jnp.sum(jnp.where(placed, route_weight[None], 0.0), axis=2)
     exp_count = lax.axis_size("exp")
     local_experts = up_weight.shape[0]
-    buffer = jnp.broadcast_to(
-        packed.reshape(1, exp_count, local_experts, capacity, model_dim),
-        (seq_count, exp_count, local_experts, capacity, model_dim),
+    packed = packed.reshape(exp_count, local_experts, capacity, model_dim)
+    summed = []
+    for expert in range(local_experts):
+        mine = lax.all_to_all(packed[:, expert], "exp", split_axis=0, concat_axis=0, tiled=True)
+        mine = mine.reshape(exp_count * capacity, model_dim)
+        rows = lax.all_gather(mine, "seq", axis=0, tiled=True)
+        partial = expert_part(rows, up_weight[expert], down_weight[expert])
+        total = lax.psum_scatter(partial, "seq", scatter_dimension=0, tiled=True)
+        total = total.reshape(exp_count, capacity, model_dim)
+        summed.append(lax.all_to_all(total, "exp", split_axis=0, concat_axis=0, tiled=True))
+    summed = jnp.stack(summed, axis=1).reshape(EXPERTS * capacity, model_dim)
+    combined = jnp.dot(
+        combiner.T, summed.astype(jnp.float32), precision=lax.Precision.HIGHEST
     )
-    buffer = buffer.reshape(seq_count * exp_count, local_experts, capacity, model_dim)
-    answered = expert_part(
-        lax.all_to_all(buffer, ("seq", "exp"), split_axis=0, concat_axis=0, tiled=True),
-        up_weight,
-        down_weight,
-    )
-    returned = lax.all_to_all(answered, ("seq", "exp"), split_axis=0, concat_axis=0, tiled=True)
-    summed = jnp.sum(
-        returned.reshape(seq_count, EXPERTS * capacity, model_dim), axis=0, dtype=jnp.float32
-    )
-    picked = jnp.take(summed, slot_index, axis=0).reshape(row_count, 2, model_dim)
-    combined = jnp.sum(picked * route_weight[:, :, None], axis=1)
     return (token_float + combined).astype(jnp.bfloat16)
 
 

time: 1040 us -> 690 us (0.66)
  blocking collectives: 366 us -> 37.7 us
  waiting for transfers between devices: 399 us -> 519 us
  local copies, waits for them, and re-layouts: 122 us -> 20.4 us
  other arithmetic: 38.4 us -> 12.2 us
  matrix products: 85.9 us -> 75 us
    all_to_all x1 -> x2, waiting for transfers between devices: 349 us -> 15.2 us  [per_device(): lax.all_to_all(total, 'exp', split_axis=0, concat_axis=0, tiled=True)]
    all_to_all x1 -> x2, blocking collectives: 343 us -> 37.7 us  [per_device(): lax.all_to_all(packed[:, expert], 'exp', split_axis=0, concat_axis=0, til...]
    reduce_scatter x0 -> x2, waiting for transfers between devices: none -> 246 us  [per_device(): total = lax.psum_scatter(partial, 'seq', scatter_dimension=0, tiled=True)]
    all_gather x1 -> x3, waiting for transfers between devices: 40.1 us -> 247 us  [the longest x2 181 us: per_device(): rows = lax.all_gather(mine, 'seq', axis=0, tiled=True)]
    convert_element_type x3 -> x0, local copies, waits for them, and re-layouts: 88.5 us -> none  [the longest x2 58.9 us: per_device(): jnp.sum(returned.reshape(seq_count, EXPERTS * capacity, model_dim), axis=...]
    all_gather x1 -> x0, blocking collectives: 22.2 us -> none  [per_device(): lax.all_gather(own_log[None].astype(jnp.bfloat16), 'seq', axis=0, tiled=T...]
    reduce_sum x2 -> x1, other arithmetic: 18.8 us -> 0.72 us  [per_device(): combiner = jnp.sum(jnp.where(placed, route_weight[None], 0.0), axis=2)]
    broadcast_in_dim x3 -> x0, local copies, waits for them, and re-layouts: 17.2 us -> none  [per_device(): jnp.broadcast_to(packed.reshape(1, exp_count, local_experts, capacity, mo...]
  transfers between devices with their start and end apart: 3 -> 8, of which waited for: 3 -> 7; matrix products, arithmetic and copies ran while one was open for 0% -> 11% of each run, Pallas kernels for 0% -> 0%
where the time goes in v1:
time: 690 us; the launch traced here: 689 us
  waiting for transfers between devices  519 us (75%)
  matrix products  75 us (11%)
  blocking collectives  37.7 us (5%)
  local copies, waits for them, and re-layouts  20.4 us (3%)
  between operations  13.5 us (2%)
  other arithmetic  12.2 us (2%)
  starting transfers between devices  11.9 us (2%)
    reduce_scatter x2, waiting for transfers between devices, per_device(): total = lax.psum_scatter(partial, 'seq', scatter_dimension=0, tiled=True)  246 us
    all_gather x2, waiting for transfers between devices, per_device(): rows = lax.all_gather(mine, 'seq', axis=0, tiled=True)  181 us
    all_gather x1, waiting for transfers between devices, per_device(): lax.all_gather(payload, 'seq', axis=0, tiled=False).astype(jnp.float32)  65.6 us
    all_to_all x2, blocking collectives, per_device(): lax.all_to_all(packed[:, expert], 'exp', split_axis=0, concat_axis=0, til...  37.7 us
    dot_general x2, matrix products, expert_part(): jnp.dot(hidden, down_weight, preferred_element_type=jnp.float32)  34.9 us
    dot_general x2, matrix products, expert_part(): jnp.dot(rows, up_weight, preferred_element_type=jnp.float32)  30.9 us
    all_to_all x2, waiting for transfers between devices, per_device(): lax.all_to_all(total, 'exp', split_axis=0, concat_axis=0, tiled=True)  15.2 us
  transfers between devices with their start and end apart: 8, of which 7 were waited for; matrix products, arithmetic and copies ran while one was open for 11% of the time, Pallas kernels for 0%

profile of v1, /device:TPU:0, one launch (start us, length us, event | category | flops | bytes accessed | tf_op | source)
XLA Modules:
  0.0 689.3 jit_solution(1766110039906723790)
XLA Ops:
  6.5 0.8 reshape.252
  7.3 0.6 reduce-window.6
  7.9 0.2 slice_reduce_fusion
  8.1 0.1 copy.108
  8.4 0.1 copy.109
  8.4 1.4 copy.110
  9.9 0.3 copy.111
  10.2 0.4 fusion.29
  10.6 0.8 fusion.35
  11.4 0.1 copy.113
  11.5 0.3 copy.114
  11.8 0.1 copy.137
  11.9 0.1 copy.122
  12.0 0.1 eq.30
  12.2 65.6 %all-gather.9.cloned.1.call-done = bf16[104,128,128]{2,1,0:T(8,128)(2,1)} async-done(((bf16[13,128,128]{2,1,0:T(8,128)(2,1)}), bf16[104,128,128]{2,1,0:T(8,128)(2,1)}) %all-gather.9.cloned.1.call-update) | async-done | bytes 3407888 | tf_op jit(solution)/shard_map/all_gather | solution.py:66
  77.8 0.7 slice_convert_fusion
  78.5 0.1 select_reduce_fusion.2
  78.6 0.1 select_bitcast_fusion
  78.7 2.6 multiply_reduce_fusion
  81.3 1.6 fusion.26
  83.0 3.8 fusion.24
  86.8 1.7 fusion.25
  88.5 0.5 copy.120
  89.0 2.2 add_convert_fusion
  91.2 3.5 all-to-all-start
  94.7 0.0 all-gather.5.cloned.1.call-start
  94.7 0.1 fusion.37
  94.8 0.2 reduce_window_sum.59
  95.0 0.2 select_reduce_fusion.1
  95.1 0.1 reduce_sum.54
  95.3 0.1 copy.123
  95.4 0.1 fusion.36
  95.5 10.8 %all-to-all-done = bf16[4,64,1536]{2,1,0:T(8,128)(2,1)S(1)} async-done(((bf16[4,64,1536]{2,1,0:T(8,128)(2,1)}), bf16[4,64,1536]{2,1,0:T(8,128)(2,1)S(1)}, u32[]{:S(2)}, u32[]{:S(2)}) %all-to-all-start) | async-done | bytes 786464 | tf_op jit(solution)/shard_map/all_to_all | solution.py:91
  106.3 0.2 convert_bitcast_fusion
  106.5 0.1 copy.139
  106.6 0.3 fusion.23
  106.9 0.3 copy-done.3
  107.2 0.7 convolution_convert_fusion
  108.0 2.1 reshape.263
  110.1 2.8 slice_bitcast_fusion.2
  112.9 18.3 %all_to_all.33 = bf16[4,20,6144]{2,1,0:T(8,128)(2,1)S(1)} all-to-all(bf16[4,20,6144]{2,1,0:T(8,128)(2,1)S(1)} %get-tuple-element.34), channel_id=1, replica_groups=mesh['seq'=8,'exp'=4] {'exp'}, dimensions={0} | all-to-all | bytes 1966080 | tf_op jit(solution)/shard_map/all_to_all | solution.py:111
  131.2 1.1 reshape.264
  132.3 19.4 %all_to_all.34 = bf16[4,20,6144]{2,1,0:T(8,128)(2,1)S(1)} all-to-all(bf16[4,20,6144]{2,1,0:T(8,128)(2,1)} %get-tuple-element.35), channel_id=1, replica_groups=mesh['seq'=8,'exp'=4] {'exp'}, dimensions={0} | all-to-all | bytes 1966080 | tf_op jit(solution)/shard_map/all_to_all | solution.py:111
  151.7 1.1 reshape.266
  152.8 0.2 reduce-scatter.3.cloned.1.call-start
  153.1 95.4 %all-gather.5.cloned.1.call-done = bf16[640,6144]{1,0:T(8,128)(2,1)} async-done(((bf16[80,6144]{1,0:T(8,128)(2,1)}), bf16[640,6144]{1,0:T(8,128)(2,1)}) %all-gather.5.cloned.1.call-update) | async-done | bytes 7864336 | tf_op jit(solution)/shard_map/all_gather | solution.py:113
  248.5 15.5 %multiply_convert_fusion.2 = bf16[640,1152]{1,0:T(8,128)(2,1)S(1)} fusion(bf16[640,6144]{1,0:T(8,128)(2,1)} %all-gather.5.cloned.1.call-done, bf16[2,6144,1152]{2,1,0:T(8,128)(2,1)} %param.22), kind=kOutput, calls=%fused_computation.21 | convolution fusion | flops 9063383040 | bytes 23494656 | tf_op jit(solution)/shard_map/dot_general | solution.py:12
  263.9 17.4 %fusion.12 = bf16[640,6144]{1,0:T(8,128)(2,1)} fusion(bf16[640,1152]{1,0:T(8,128)(2,1)S(1)} %multiply_convert_fusion.2, bf16[2,1152,6144]{2,1,0:T(8,128)(2,1)} %param.23), kind=kOutput, calls=%fused_computation.12 | convolution fusion | flops 9063628800 | bytes 23494656 | tf_op jit(solution)/shard_map/dot_general | solution.py:15
  281.4 0.3 reduce-scatter.5.cloned.1.call-start
  281.6 85.7 %all-gather.7.cloned.1.call-done = bf16[640,6144]{1,0:T(8,128)(2,1)} async-done(((bf16[80,6144]{1,0:T(8,128)(2,1)}), bf16[640,6144]{1,0:T(8,128)(2,1)}) %all-gather.7.cloned.1.call-update) | async-done | bytes 7864336 | tf_op jit(solution)/shard_map/all_gather | solution.py:113
  367.3 15.5 %multiply_convert_fusion.1 = bf16[640,1152]{1,0:T(8,128)(2,1)S(1)} fusion(bf16[640,6144]{1,0:T(8,128)(2,1)} %all-gather.7.cloned.1.call-done, bf16[2,6144,1152]{2,1,0:T(8,128)(2,1)} %param.22), kind=kOutput, calls=%fused_computation.20 | convolution fusion | flops 9063383040 | bytes 23494656 | tf_op jit(solution)/shard_map/dot_general | solution.py:12
  382.7 17.5 %fusion.15 = bf16[640,6144]{1,0:T(8,128)(2,1)} fusion(bf16[640,1152]{1,0:T(8,128)(2,1)S(1)} %multiply_convert_fusion.1, bf16[2,1152,6144]{2,1,0:T(8,128)(2,1)} %param.23), kind=kOutput, calls=%fused_computation.13 | convolution fusion | flops 9063628800 | bytes 23494656 | tf_op jit(solution)/shard_map/dot_general | solution.py:15
  400.3 108.8 %reduce-scatter.3.cloned.1.call-done = bf16[80,6144]{1,0:T(8,128)(2,1)} async-done(((bf16[640,6144]{1,0:T(8,128)(2,1)}), bf16[80,6144]{1,0:T(8,128)(2,1)}) %reduce-scatter.3.cloned.1.call-update) | async-done | bytes 983056 | tf_op jit(solution)/shard_map/reduce_scatter | solution.py:115
  509.0 2.3 reshape.265
  511.3 3.5 all-to-all-start.2
  514.9 137.1 %reduce-scatter.5.cloned.1.call-done = bf16[80,6144]{1,0:T(8,128)(2,1)} async-done(((bf16[640,6144]{1,0:T(8,128)(2,1)}), bf16[80,6144]{1,0:T(8,128)(2,1)}) %reduce-scatter.5.cloned.1.call-update) | async-done | bytes 983056 | tf_op jit(solution)/shard_map/reduce_scatter | solution.py:115
  652.0 2.2 reshape.267
  654.2 4.3 all-to-all-start.4
  658.5 0.7 select_reduce_fusion
  659.2 15.2 %all-to-all-done.4 = bf16[4,20,6144]{2,1,0:T(8,128)(2,1)} async-done(((bf16[4,20,6144]{2,1,0:T(8,128)(2,1)}), bf16[4,20,6144]{2,1,0:T(8,128)(2,1)}, u32[]{:S(2)}, u32[]{:S(2)}) %all-to-all-start.4) | async-done | bytes 983072 | tf_op jit(solution)/shard_map/all_to_all | solution.py:117
  674.4 1.6 pad_maximum_fusion
  675.9 1.6 copy.124
  677.5 2.6 reshape.268
  680.1 2.6 fusion.18
  (44 shorter events, 0.4 us)
Async XLA Ops:
  6.5 3.3 copy-start
  6.5 71.2 %all-gather.9.cloned.1.call-start = ((), (), s32[]{:S(2)}) async-start(), calls=%async_computation.11 | async-start | bytes 3833856 | tf_op jit(solution)/shard_map/all_gather | solution.py:66
  9.9 1.6 copy-start.1
  10.2 1.6 copy-start.2
  10.2 1.8 copy-start.7
  83.0 3.8 copy-start.6
  91.2 15.1 %all-to-all-start = ((bf16[4,64,1536]{2,1,0:T(8,128)(2,1)}), bf16[4,64,1536]{2,1,0:T(8,128)(2,1)S(1)}, u32[]{:S(2)}, u32[]{:S(2)}) async-start(bf16[4,64,1536]{2,1,0:T(8,128)(2,1)} %bitcast.23), calls=%async_computation | async-start | bytes 1572864 | tf_op jit(solution)/shard_map/all_to_all | solution.py:91
  94.7 153.8 %all-gather.5.cloned.1.call-start = ((), (), s32[]{:S(2)}) async-start(), calls=%async_computation.7 | async-start | bytes 8847360 | tf_op jit(solution)/shard_map/all_gather | solution.py:113
  95.4 11.2 %copy-start.4 = (s32[64,2]{0,1:T(2,128)}, s32[64,2]{0,1:T(2,128)S(1)}, u32[]{:S(2)}) copy-start(s32[64,2]{0,1:T(2,128)S(1)} %multiply_add_fusion) | copy-start | bytes 1540
  106.5 0.7 copy-start.3
  132.3 235.0 %all-gather.7.cloned.1.call-start = ((), (), s32[]{:S(2)}) async-start(), calls=%async_computation.9 | async-start | bytes 8847360 | tf_op jit(solution)/shard_map/all_gather | solution.py:113
  152.8 356.2 %reduce-scatter.3.cloned.1.call-start = ((), (), s32[]{:S(2)}) async-start(), calls=%async_computation.8 | async-start | bytes 8847360 | tf_op jit(solution)/shard_map/reduce_scatter | solution.py:115
  281.4 370.6 %reduce-scatter.5.cloned.1.call-start = ((), (), s32[]{:S(2)}) async-start(), calls=%async_computation.10 | async-start | bytes 8847360 | tf_op jit(solution)/shard_map/reduce_scatter | solution.py:115
  511.3 142.9 %all-to-all-start.2 = ((bf16[4,20,6144]{2,1,0:T(8,128)(2,1)}), bf16[4,20,6144]{2,1,0:T(8,128)(2,1)S(1)}, u32[]{:S(2)}, u32[]{:S(2)}) async-start(bf16[4,20,6144]{2,1,0:T(8,128)(2,1)} %reshape.265), calls=%async_computation.3 | async-start | bytes 2359296 | tf_op jit(solution)/shard_map/all_to_all | solution.py:117
  514.8 143.6 %copy-start.5 = (s32[64,2]{0,1:T(2,128)S(1)}, s32[64,2]{0,1:T(2,128)}, u32[]{:S(2)}) copy-start(s32[64,2]{0,1:T(2,128)} %copy-done.4) | copy-start | bytes 1540
  514.8 143.6 %copy-start.8 = (f32[64,2]{0,1:T(2,128)S(1)}, f32[64,2]{0,1:T(2,128)}, u32[]{:S(2)}) copy-start(f32[64,2]{0,1:T(2,128)} %param.21) | copy-start | bytes 1540
  654.2 20.2 %all-to-all-start.4 = ((bf16[4,20,6144]{2,1,0:T(8,128)(2,1)}), bf16[4,20,6144]{2,1,0:T(8,128)(2,1)}, u32[]{:S(2)}, u32[]{:S(2)}) async-start(bf16[4,20,6144]{2,1,0:T(8,128)(2,1)} %reshape.267), calls=%async_computation.6 | async-start | bytes 2359296 | tf_op jit(solution)/shard_map/all_to_all | solution.py:117
Sparse Core Ops, SparseCore 0:
  11.5 66.2 all-gather.8
  132.4 116.0 all-gather.4
  250.7 116.5 all-gather.6
  370.8 138.2 reduce-scatter.2
  512.5 139.4 reduce-scatter.4

commit v2 on v1

--- a/solution.py
+++ b/solution.py
@@ -1,11 +1,286 @@
 import jax
 import jax.numpy as jnp
 from jax import lax
+from jax.experimental import pallas as pl
+from jax.experimental.pallas import tpu as pltpu
 from jax.sharding import PartitionSpec as P
 
 HEAD_DIM = 128
 BLK = 256
 EXPERTS = 8
+
+
+MESH = pl.DeviceIdType.MESH
+Z_LEN = 4
+
+
+def chip_place():
+    seq, exp = lax.axis_index("seq"), lax.axis_index("exp")
+    z, y, x, c = lax.div(seq, 2), lax.rem(seq, 2), lax.div(exp, 2), lax.rem(exp, 2)
+
+    def block(shift, jy, jx, jc):
+        zz = lax.rem(z + shift + Z_LEN, Z_LEN)
+        yy, xx, cc = lax.rem(y + jy, 2), lax.rem(x + jx, 2), lax.rem(c + jc, 2)
+        return (zz * 2 + yy) * 4 + xx * 2 + cc
+
+    def device(shift, jy, jx, jc):
+        index = block(shift, jy, jx, jc)
+        return (lax.div(index, 4), lax.rem(index, 4))
+
+    return block, device
+
+
+def greet(device):
+    barrier = pltpu.get_barrier_semaphore()
+    peers = [device(1, 0, 0, 0), device(2, 0, 0, 0), device(3, 0, 0, 0)]
+    peers += [device(0, 1, 0, 0), device(0, 0, 1, 0), device(0, 0, 0, 1)]
+    for peer in peers:
+        pl.semaphore_signal(barrier, inc=1, device_id=peer, device_id_type=MESH)
+    pl.semaphore_wait(barrier, len(peers))
+
+
+def gather_kernel(own_ref, out_ref, send_sem, recv_sem, local_sem):
+    block, device = chip_place()
+    half = own_ref.shape[1] // 2
+    left, right = pl.ds(0, half), pl.ds(half, half)
+    greet(device)
+    copies = {}
+
+    def send(name, src, dst, peer):
+        spot = len(copies)
+        copies[name] = pltpu.make_async_remote_copy(
+            src_ref=src,
+            dst_ref=dst,
+            send_sem=send_sem.at[spot],
+            recv_sem=recv_sem.at[spot],
+            device_id=peer,
+            device_id_type=MESH,
+        )
+        copies[name].start()
+
+    y_peer, x_peer, twin = device(0, 1, 0, 0), device(0, 0, 1, 0), device(0, 0, 0, 1)
+    mine = out_ref.at[block(0, 0, 0, 0)]
+    keep = pltpu.make_async_copy(own_ref, mine, local_sem)
+    keep.start()
+
+    def spread_diagonal(k):
+        there = out_ref.at[block(-k, 1, 1, 0)]
+        copies["da", k].wait_recv()
+        send(("ta", k), there.at[:, left], there.at[:, left], twin)
+        copies["db", k].wait_recv()
+        send(("tb", k), there.at[:, right], there.at[:, right], twin)
+
+    order = (0, 1, 3, 2)
+    for turn, k in enumerate(order):
+        spot = out_ref.at[block(-k, 0, 0, 0)]
+        if k:
+            copies["z", k].wait_recv()
+        src = spot if k else own_ref
+        send(("y", k), src, spot, y_peer)
+        send(("x", k), src, spot, x_peer)
+        if turn + 1 < len(order):
+            later = order[turn + 1]
+            send(("z", later), own_ref, mine, device(later, 0, 0, 0))
+        send(("t", k), src, spot, twin)
+        if turn:
+            spread_diagonal(order[turn - 1])
+        from_y = out_ref.at[block(-k, 1, 0, 0)]
+        from_x = out_ref.at[block(-k, 0, 1, 0)]
+        copies["y", k].wait_recv()
+        send(("da", k), from_y.at[:, left], from_y.at[:, left], x_peer)
+        copies["x", k].wait_recv()
+        send(("db", k), from_x.at[:, right], from_x.at[:, right], y_peer)
+        send(("ty", k), from_y, from_y, twin)
+        send(("tx", k), from_x, from_x, twin)
+    spread_diagonal(order[-1])
+    for name, copy in copies.items():
+        copy.wait_send()
+        if name[0] in ("t", "ty", "tx", "ta", "tb"):
+            copy.wait_recv()
+    keep.wait()
+
+
+def gather_rows(rows, block_total):
+    row_count, width = rows.shape
+    return pl.pallas_call(
+        gather_kernel,
+        out_shape=jax.ShapeDtypeStruct((block_total, row_count, width), rows.dtype),
+        in_specs=[pl.BlockSpec(memory_space=pl.ANY)],
+        out_specs=pl.BlockSpec(memory_space=pl.ANY),
+        scratch_shapes=[
+            pltpu.SemaphoreType.DMA((39,)),
+            pltpu.SemaphoreType.DMA((39,)),
+            pltpu.SemaphoreType.DMA,
+        ],
+        compiler_params=pltpu.CompilerParams(collective_id=0, has_side_effects=True),
+        name="gather_rows",
+    )(rows)
+
+
+def reduce_kernel(part_ref, out_ref, mine, twin_in, diag_in, y_in, x_in, z_in, send_sem, recv_sem, load_sem):
+    block, device = chip_place()
+    row_count, width = out_ref.shape
+    half = width // 2
+    full, left, right = pl.ds(0, width), pl.ds(0, half), pl.ds(half, half)
+    tile = 16
+    greet(device)
+    copies = {}
+
+    def send(name, src, dst, peer):
+        spot = len(copies)
+        copies[name] = pltpu.make_async_remote_copy(
+            src_ref=src,
+            dst_ref=dst,
+            send_sem=send_sem.at[spot],
+            recv_sem=recv_sem.at[spot],
+            device_id=peer,
+            device_id_type=MESH,
+        )
+        copies[name].start()
+
+    def add_into(target, sources, columns):
+        @pl.loop(0, row_count // tile)
+        def _(step):
+            rows = pl.ds(step * tile, tile)
+            total = target[rows, columns].astype(jnp.float32)
+            for source in sources:
+                total = total + source[rows, columns].astype(jnp.float32)
+            target[rows, columns] = total.astype(target.dtype)
+
+    y_peer, x_peer, twin = device(0, 1, 0, 0), device(0, 0, 1, 0), device(0, 0, 0, 1)
+    order = (2, 1, 3, 0)
+    loads = {}
+    for turn, k in enumerate(order):
+        for q in (3, 2, 1, 0):
+            spot = turn * 4 + q
+            theirs = part_ref.at[block(k, q // 2, q % 2, 1)]
+            send(("t", spot), theirs, twin_in.at[spot], twin)
+            loads[spot] = pltpu.make_async_copy(
+                part_ref.at[block(k, q // 2, q % 2, 0)], mine.at[spot], load_sem.at[spot]
+            )
+            loads[spot].start()
+
+    def join_twin(turn):
+        for q in (3, 2, 1, 0):
+            spot = turn * 4 + q
+            loads[spot].wait()
+            copies["t", spot].wait_recv()
+            add_into(mine.at[spot], [twin_in.at[spot]], full)
+            if q == 3:
+                source, target = mine.at[spot], diag_in.at[turn]
+                send(("da", turn), source.at[:, left], target.at[:, left], x_peer)
+                send(("db", turn), source.at[:, right], target.at[:, right], y_peer)
+
+    def join_diagonal(turn):
+        copies["da", turn].wait_recv()
+        add_into(mine.at[turn * 4 + 2], [diag_in.at[turn]], left)
+        send(("y", turn), mine.at[turn * 4 + 2], y_in.at[turn], y_peer)
+        copies["db", turn].wait_recv()
+        add_into(mine.at[turn * 4 + 1], [diag_in.at[turn]], right)
+        send(("x", turn), mine.at[turn * 4 + 1], x_in.at[turn], x_peer)
+
+    def join_sides(turn):
+        copies["y", turn].wait_recv()
+        copies["x", turn].wait_recv()
+        add_into(mine.at[turn * 4], [y_in.at[turn], x_in.at[turn]], full)
+        if order[turn]:
+            send(("z", turn), mine.at[turn * 4], z_in.at[turn], device(order[turn], 0, 0, 0))
+
+    for turn in range(len(order) + 2):
+        if turn < len(order):
+            join_twin(turn)
+        if 0 <= turn - 1 < len(order):
+            join_diagonal(turn - 1)
+        if 0 <= turn - 2:
+            join_sides(turn - 2)
+    for turn in range(3):
+        copies["z", turn].wait_recv()
+    last = mine.at[12]
+
+    @pl.loop(0, row_count // tile)
+    def _(step):
+        rows = pl.ds(step * tile, tile)
+        total = last[rows, :].astype(jnp.float32)
+        for turn in range(3):
+            total = total + z_in[turn, rows, :].astype(jnp.float32)
+        out_ref[rows, :] = total
+
+    for copy in copies.values():
+        copy.wait_send()
+
+
+def reduce_rows(parts):
+    block_total, row_count, width = parts.shape
+    many = lambda n: pltpu.VMEM((n, row_count, width), parts.dtype)
+    return pl.pallas_call(
+        reduce_kernel,
+        out_shape=jax.ShapeDtypeStruct((row_count, width), jnp.float32),
+        in_specs=[pl.BlockSpec(memory_space=pl.ANY)],
+        out_specs=pl.BlockSpec(memory_space=pltpu.VMEM),
+        scratch_shapes=[
+            many(16),
+            many(16),
+            many(4),
+            many(4),
+            many(4),
+            many(3),
+            pltpu.SemaphoreType.DMA((35,)),
+            pltpu.SemaphoreType.DMA((35,)),
+            pltpu.SemaphoreType.DMA((16,)),
+        ],
+        compiler_params=pltpu.CompilerParams(
+            collective_id=1, has_side_effects=True, vmem_limit_bytes=56 * 1024 * 1024
+        ),
+        name="reduce_rows",
+    )(parts)
+
+
+def experts_by_kernels(norm_rows, routes, route_weight, up_weight, down_weight, capacity):
+    row_count, model_dim = norm_rows.shape
+    seq_count, exp_count = lax.axis_size("seq"), lax.axis_size("exp")
+    block_total = seq_count * exp_count
+    local_experts = up_weight.shape[0]
+    sheet = jnp.concatenate([routes.astype(jnp.float32), route_weight], axis=1).T
+    sheets = lax.all_gather(sheet, ("seq", "exp"), axis=0, tiled=False)
+    first = lax.axis_index("exp") * local_experts
+    local_ids = (first + jnp.arange(local_experts)).astype(jnp.float32)[:, None, None, None]
+    hits = sheets[None, :, :2] == local_ids
+    member = jnp.any(hits, axis=2)
+    member_weight = jnp.sum(jnp.where(hits, sheets[None, :, 2:], 0.0), axis=2)
+    earlier = jnp.triu(jnp.ones((row_count, row_count), jnp.bfloat16), 1)
+    rank = jnp.einsum(
+        "lbt,tu->lbu",
+        member.astype(jnp.bfloat16),
+        earlier,
+        preferred_element_type=jnp.float32,
+    ).astype(jnp.int32)
+    slot = rank + (jnp.arange(block_total, dtype=jnp.int32) % exp_count)[None, :, None] * capacity
+    grouped = (local_experts, seq_count, 1, exp_count * row_count)
+    slots = exp_count * capacity
+    pick = (jnp.arange(slots, dtype=jnp.int32)[:, None] == slot.reshape(grouped)) & member.reshape(
+        grouped
+    )
+    slot_weight = jnp.sum(jnp.where(pick, member_weight.reshape(grouped), 0.0), axis=3)
+    pick = pick.astype(jnp.bfloat16)
+    rows = gather_rows(norm_rows, block_total)
+    rows = rows.reshape(seq_count, exp_count * row_count, model_dim)
+    parts = []
+    for expert in range(local_experts):
+        packed = jnp.einsum(
+            "gst,gtd->gsd", pick[expert], rows, preferred_element_type=jnp.float32
+        ).astype(jnp.bfloat16)
+        packed = packed.reshape(seq_count * slots, model_dim)
+        hidden = jax.nn.silu(
+            jnp.dot(packed, up_weight[expert], preferred_element_type=jnp.float32)
+        ).astype(jnp.bfloat16)
+        part = jnp.dot(hidden, down_weight[expert], preferred_element_type=jnp.float32)
+        part = (part * slot_weight[expert].reshape(-1, 1)).astype(jnp.bfloat16)
+        parts.append(part.reshape(seq_count, slots, model_dim))
+    spread = sum(
+        jnp.einsum("gst,gsd->gtd", pick[expert], parts[expert], preferred_element_type=jnp.float32)
+        for expert in range(local_experts)
+    ).astype(jnp.bfloat16)
+    return reduce_rows(spread.reshape(block_total, row_count, model_dim))
 
 
 def expert_part(rows, up_weight, down_weight):
@@ -94,6 +369,11 @@
     row_square = jnp.mean(token_float * token_float, axis=-1, keepdims=True)
     norm_rows = (token_float * lax.rsqrt(row_square + 1e-06) * moe_gain).astype(jnp.bfloat16)
     capacity = row_count * 10 // (4 * EXPERTS)
+    if (lax.axis_size("seq"), lax.axis_size("exp")) == (2 * Z_LEN, 4):
+        combined = experts_by_kernels(
+            norm_rows, routes, route_weight, up_weight, down_weight, capacity
+        )
+        return (token_float + combined).astype(jnp.bfloat16)
     flat_ids = routes.reshape(-1)
     onehot = (flat_ids[:, None] == jnp.arange(EXPERTS, dtype=jnp.int32)[None, :]).astype(jnp.int32)
     slot_rank = jnp.sum((jnp.cumsum(onehot, axis=0) - 1) * onehot, axis=1)

time: 690 us -> 494 us (0.72)
  waiting for transfers between devices: 519 us -> 32.2 us
  Pallas kernels: 0 us -> 223 us
  matrix products: 75 us -> 152 us
  local copies, waits for them, and re-layouts: 20.4 us -> 5.64 us
  starting transfers between devices: 11.9 us -> 3.67 us
    reduce_scatter x2 -> x0, waiting for transfers between devices: 246 us -> none  [per_device(): total = lax.psum_scatter(partial, 'seq', scatter_dimension=0, tiled=True)]
    pallas_call x0 -> x2, Pallas kernels: none -> 223 us  [the longest x1 112 us: gather_rows(): pl.pallas_call(gather_kernel, out_shape=jax.ShapeDtypeStruct((block_total...]
    all_gather x2 -> x0, waiting for transfers between devices: 181 us -> none  [per_device(): rows = lax.all_gather(mine, 'seq', axis=0, tiled=True)]
    dot_general x6 -> x9, matrix products: 69.2 us -> 146 us  [the longest x2 50.7 us: experts_by_kernels(): jnp.einsum('gst,gsd->gtd', pick[expert], parts[expert], preferred_element...]
    all_gather x1, waiting for transfers between devices: 65.6 us -> 21.4 us  [per_device(): lax.all_gather(payload, 'seq', axis=0, tiled=False).astype(jnp.float32)]
    all_gather x0 -> x1, blocking collectives: none -> 43.9 us  [experts_by_kernels(): sheets = lax.all_gather(sheet, ('seq', 'exp'), axis=0, tiled=False)]
    all_to_all x2 -> x0, blocking collectives: 37.7 us -> none  [per_device(): lax.all_to_all(packed[:, expert], 'exp', split_axis=0, concat_axis=0, til...]
    all_to_all x2 -> x0, waiting for transfers between devices: 15.2 us -> none  [per_device(): lax.all_to_all(total, 'exp', split_axis=0, concat_axis=0, tiled=True)]
  transfers between devices with their start and end apart: 8 -> 2, of which waited for: 7 -> 2; matrix products, arithmetic and copies ran while one was open for 11% -> 0% of each run, Pallas kernels for 0% -> 0%
where the time goes in v2:
time: 494 us; the launch traced here: 488 us
  Pallas kernels  223 us (45%)
  matrix products  152 us (31%)
  blocking collectives  43.9 us (9%)
  waiting for transfers between devices  32.2 us (7%)
  between operations  14.2 us (3%)
  other arithmetic  13.7 us (3%)
  local copies, waits for them, and re-layouts  5.64 us (1%)
    pallas_call x1, Pallas kernels, gather_rows(): pl.pallas_call(gather_kernel, out_shape=jax.ShapeDtypeStruct((block_total...  112 us
    pallas_call x1, Pallas kernels, reduce_rows(): pl.pallas_call(reduce_kernel, out_shape=jax.ShapeDtypeStruct((row_count,...  111 us
    dot_general x2, matrix products, experts_by_kernels(): jnp.einsum('gst,gsd->gtd', pick[expert], parts[expert], preferred_element...  50.7 us
    all_gather x1, blocking collectives, experts_by_kernels(): sheets = lax.all_gather(sheet, ('seq', 'exp'), axis=0, tiled=False)  43.9 us
    dot_general x2, matrix products, experts_by_kernels(): jnp.dot(hidden, down_weight[expert], preferred_element_type=jnp.float32)  34.7 us
    dot_general x2, matrix products, experts_by_kernels(): jnp.einsum('gst,gtd->gsd', pick[expert], rows, preferred_element_type=jnp...  31.3 us
    dot_general x2, matrix products, experts_by_kernels(): jnp.dot(packed, up_weight[expert], preferred_element_type=jnp.float32)  29.6 us
    all_gather x1, waiting for transfers between devices, per_device(): lax.all_gather(payload, 'seq', axis=0, tiled=False).astype(jnp.float32)  21.4 us
  transfers between devices with their start and end apart: 2, of which 2 were waited for; matrix products, arithmetic and copies ran while one was open for 0% of the time, Pallas kernels for 0%

profile of v2, /device:TPU:0, one launch (start us, length us, event | category | flops | bytes accessed | tf_op | source)
XLA Modules:
  0.0 488.2 jit_solution(16598610567221570461)
XLA Ops:
  6.5 0.0 all-gather.5.cloned.1.call-start
  6.5 0.8 reshape.258
  7.3 0.6 reduce-window.6
  7.9 0.2 slice_reduce_fusion
  8.1 0.1 copy.69
  8.4 0.1 copy.70
  8.4 1.4 copy.71
  9.9 0.0 copy-done.3
  9.9 0.0 copy-start.4
  9.9 0.3 copy.72
  10.2 0.0 copy-start.5
  10.2 0.4 fusion.27
  10.6 0.8 fusion.33
  11.4 0.0 all-gather.5.cloned.1.call-update
  11.4 0.0 copy-done.8
  11.5 0.0 copy-done.9
  11.5 43.9 %all-gather.2 = f32[32,4,64]{2,1,0:T(4,128)S(1)} all-gather(f32[1,4,64]{2,1,0:T(4,128)S(1)} %maximum_bitcast_fusion), channel_id=3, replica_groups=mesh['seq'=8,'exp'=4] {'seq','exp'}, dimensions={0}, use_global_device_ids=true | all-gather | bytes 33792 | tf_op jit(solution)/shard_map/all_gather | solution.py:244
  55.5 0.1 fusion.34
  55.6 0.1 broadcast_in_dim.108
  55.7 0.1 compare_reduce_fusion
  55.8 0.1 and.28
  55.9 0.1 fusion.28
  55.9 0.1 eq.34
  56.1 0.1 copy.97
  56.2 0.1 copy.74
  56.3 0.0 copy-done.4
  56.3 0.3 copy.75
  56.6 21.4 %all-gather.5.cloned.1.call-done = bf16[104,128,128]{2,1,0:T(8,128)(2,1)} async-done(((bf16[13,128,128]{2,1,0:T(8,128)(2,1)}), bf16[104,128,128]{2,1,0:T(8,128)(2,1)}) %all-gather.5.cloned.1.call-update) | async-done | bytes 3407888 | tf_op jit(solution)/shard_map/all_gather | solution.py:341
  78.0 0.7 slice_convert_fusion
  78.7 0.1 select_reduce_fusion.1
  78.8 0.1 select_bitcast_fusion
  78.9 2.6 multiply_reduce_fusion
  81.5 0.0 copy-done.5
  81.5 1.6 fusion.23
  83.2 0.0 copy-start.7
  83.2 3.8 fusion.21
  87.0 0.0 copy-done.7
  87.0 1.7 fusion.22
  88.7 0.5 copy.81
  89.1 2.2 add_convert_fusion.2
  91.3 3.7 all-to-all-start
  95.0 0.4 select_reduce_fusion
  95.4 0.1 mul.154
  95.5 0.1 mul.150
  95.5 0.2 fusion.26
  95.8 0.0 copy-start.6
  95.8 10.8 %all-to-all-done = bf16[4,64,1536]{2,1,0:T(8,128)(2,1)S(1)} async-done(((bf16[4,64,1536]{2,1,0:T(8,128)(2,1)}), bf16[4,64,1536]{2,1,0:T(8,128)(2,1)S(1)}, u32[]{:S(2)}, u32[]{:S(2)}) %all-to-all-start) | async-done | bytes 786464 | tf_op jit(solution)/shard_map/all_to_all | solution.py:366
  106.6 0.3 fusion.20
  106.9 0.2 convert_bitcast_fusion
  107.1 0.1 copy.99
  107.2 1.2 copy-done
  108.4 1.1 multiply_convert_fusion.5.own_ref
  109.5 111.6 %gather_rows.1 = bf16[32,64,6144]{2,1,0:T(8,128)(2,1)} custom-call(bf16[64,6144]{1,0:T(8,128)(2,1)} %multiply_convert_fusion.5.own_ref), custom_call_target="tpu_custom_call" | custom-call | tf_op jit(solution)/shard_map/gather_rows/pallas_call | solution.py:105
  221.0 15.7 %convolution_convert_fusion = bf16[8,80,6144]{2,1,0:T(8,128)(2,1)} fusion(bf16[8,256,6144]{2,1,0:T(8,128)(2,1)} %bitcast.114, pred[2,8,80,256]{3,2,1,0:T(8,128)(4,1)S(1)} %fusion.26), kind=kOutput, calls=%fused_computation.15 | convolution fusion | flops 2017198080 | bytes 33193984 | tf_op jit(solution)/shard_map/gst,gtd->gsd/dot_general | solution.py:269
  236.7 15.6 %convolution_convert_fusion.1 = bf16[8,80,6144]{2,1,0:T(8,128)(2,1)} fusion(bf16[8,256,6144]{2,1,0:T(8,128)(2,1)} %bitcast.115, pred[2,8,80,256]{3,2,1,0:T(8,128)(4,1)S(1)} %fusion.26), kind=kOutput, calls=%fused_computation.16 | convolution fusion | flops 2017198080 | bytes 33193984 | tf_op jit(solution)/shard_map/gst,gtd->gsd/dot_general | solution.py:269
  252.3 15.8 %multiply_convert_fusion.4 = bf16[640,1152]{1,0:T(8,128)(2,1)S(1)} fusion(bf16[640,6144]{1,0:T(8,128)(2,1)} %bitcast.122, bf16[2,6144,1152]{2,1,0:T(8,128)(2,1)} %param.22), kind=kOutput, calls=%fused_computation.21 | convolution fusion | flops 9063383040 | bytes 23494656 | tf_op jit(solution)/shard_map/dot_general | solution.py:274
  268.1 0.0 copy-done.2
  268.1 13.9 %multiply_convert_fusion.3 = bf16[640,1152]{1,0:T(8,128)(2,1)S(1)} fusion(bf16[640,6144]{1,0:T(8,128)(2,1)S(1)} %bitcast.120, bf16[2,6144,1152]{2,1,0:T(8,128)(2,1)} %param.22), kind=kOutput, calls=%fused_computation.20 | convolution fusion | flops 9063383040 | bytes 23494656 | tf_op jit(solution)/shard_map/dot_general | solution.py:274
  282.0 17.4 %multiply_convert_fusion.1 = bf16[640,6144]{1,0:T(8,128)(2,1)} fusion(bf16[640,1152]{1,0:T(8,128)(2,1)S(1)} %multiply_convert_fusion.4, bf16[2,1152,6144]{2,1,0:T(8,128)(2,1)} %param.23, f32[640]{0:T(1024)S(1)} %mul.150), kind=kOutput, calls=%fused_computation.2 | convolution fusion | flops 9067560960 | bytes 23497216 | tf_op jit(solution)/shard_map/dot_general | solution.py:276
  299.4 22.8 %fusion.32 = f32[8,256,6144]{2,1,0:T(8,128)} fusion(bf16[8,80,6144]{2,1,0:T(8,128)(2,1)} %bitcast.119, pred[2,8,80,256]{3,2,1,0:T(8,128)(4,1)S(1)} %fusion.26), kind=kOutput, calls=%fused_computation.50 | convolution fusion | flops 2013265920 | bytes 58359808 | tf_op jit(solution)/shard_map/gst,gsd->gtd/dot_general | solution.py:280
  322.2 17.3 %multiply_convert_fusion = bf16[640,6144]{1,0:T(8,128)(2,1)} fusion(bf16[640,1152]{1,0:T(8,128)(2,1)S(1)} %multiply_convert_fusion.3, bf16[2,1152,6144]{2,1,0:T(8,128)(2,1)} %param.23, f32[640]{0:T(1024)S(1)} %mul.154), kind=kOutput, calls=%fused_computation.1 | convolution fusion | flops 9067560960 | bytes 23497216 | tf_op jit(solution)/shard_map/dot_general | solution.py:276
  339.5 27.9 %add_convert_fusion = bf16[8,256,6144]{2,1,0:T(8,128)(2,1)} fusion(f32[8,256,6144]{2,1,0:T(8,128)} %fusion.32, bf16[8,80,6144]{2,1,0:T(8,128)(2,1)} %bitcast.121, pred[2,8,80,256]{3,2,1,0:T(8,128)(4,1)S(1)} %fusion.26), kind=kOutput, calls=%fused_computation | convolution fusion | flops 2038431744 | bytes 83525632 | tf_op jit(solution)/shard_map/gst,gsd->gtd/dot_general | solution.py:280
  367.4 111.1 %reduce_rows.1 = f32[64,6144]{1,0:T(8,128)} custom-call(bf16[32,64,6144]{2,1,0:T(8,128)(2,1)} %bitcast.116), custom_call_target="tpu_custom_call" | custom-call | tf_op jit(solution)/shard_map/reduce_rows/pallas_call | solution.py:215
  478.5 2.4 add_convert_fusion.1
  (34 shorter events, 0.3 us)
Async XLA Ops:
  6.5 3.4 copy-start.3
  6.5 71.4 %all-gather.5.cloned.1.call-start = ((), (), s32[]{:S(2)}) async-start(), calls=%async_computation.1 | async-start | bytes 3833856 | tf_op jit(solution)/shard_map/all_gather | solution.py:341
  8.4 3.0 copy-start.8
  8.4 3.0 copy-start.9
  9.9 46.4 %copy-start.4 = (bf16[256,1536]{1,0:T(8,128)(2,1)S(1)}, bf16[256,1536]{1,0:T(8,128)(2,1)}, u32[]{:S(2)}) copy-start(bf16[256,1536]{1,0:T(8,128)(2,1)} %param.13) | copy-start | bytes 2359300
  10.2 71.4 %copy-start.5 = (bf16[256,1536]{0,1:T(8,128)(2,1)}, bf16[256,1536]{0,1:T(8,128)(2,1)S(1)}, u32[]{:S(2)}) copy-start(bf16[256,1536]{0,1:T(8,128)(2,1)S(1)} %copy.72) | copy-start | bytes 2359300
  83.2 3.8 copy-start.7
  91.3 15.3 %all-to-all-start = ((bf16[4,64,1536]{2,1,0:T(8,128)(2,1)}), bf16[4,64,1536]{2,1,0:T(8,128)(2,1)S(1)}, u32[]{:S(2)}, u32[]{:S(2)}) async-start(bf16[4,64,1536]{2,1,0:T(8,128)(2,1)} %bitcast.23), calls=%async_computation | async-start | bytes 1572864 | tf_op jit(solution)/shard_map/all_to_all | solution.py:366
  95.8 12.6 %copy-start.6 = (f32[6144]{0:T(1024)S(1)}, f32[6144]{0:T(1024)}, u32[]{:S(2)}) copy-start(f32[6144]{0:T(1024)} %param.19) | copy-start | bytes 73732
  107.2 1.2 copy-start
  252.3 15.8 %copy-start.2 = (bf16[8,80,6144]{2,1,0:T(8,128)(2,1)S(1)}, bf16[8,80,6144]{2,1,0:T(8,128)(2,1)}, u32[]{:S(2)}) copy-start(bf16[8,80,6144]{2,1,0:T(8,128)(2,1)} %convolution_convert_fusion) | copy-start | bytes 23592964
  367.4 111.1 %copy-start.1 = (f32[4,8,8,1536]{3,2,0,1:T(8,128)S(1)}, f32[4,8,8,1536]{3,2,0,1:T(8,128)}, u32[]{:S(2)}) copy-start(f32[4,8,8,1536]{3,2,0,1:T(8,128)} %copy-done) | copy-start | bytes 4718596
Sparse Core Ops, SparseCore 0:
  11.5 66.4 all-gather.4

commit v3 on v2

--- a/solution.py
+++ b/solution.py
@@ -39,7 +39,21 @@
     pl.semaphore_wait(barrier, len(peers))
 
 
-def gather_kernel(own_ref, out_ref, send_sem, recv_sem, local_sem):
+def gather_up_kernel(
+    own_ref,
+    share_ref,
+    weight_ref,
+    out_ref,
+    hidden_ref,
+    weights,
+    rows_in,
+    total,
+    send_sem,
+    recv_sem,
+    local_sem,
+    load_sem,
+    weight_sem,
+):
     block, device = chip_place()
     half = own_ref.shape[1] // 2
     left, right = pl.ds(0, half), pl.ds(half, half)
@@ -62,6 +76,50 @@
     mine = out_ref.at[block(0, 0, 0, 0)]
     keep = pltpu.make_async_copy(own_ref, mine, local_sem)
     keep.start()
+
+    expert_count, depth, hidden_width = weight_ref.shape
+    weight_copy = pltpu.make_async_copy(weight_ref, weights, weight_sem)
+    row_count = own_ref.shape[0]
+    step_depth = 512
+
+    def compute(k, jy):
+        names = [("ty", k), ("ta", k), ("tb", k)] if jy else [("t", k), ("tx", k)]
+        for name in names:
+            copies[name].wait_recv()
+        if (k, jy) == (0, 0):
+            weight_copy.wait()
+            keep.wait()
+        spots = [block(-k, jy, jx, jc) for jx in range(2) for jc in range(2)]
+        loads = []
+        for place, spot in enumerate(spots):
+            load = pltpu.make_async_copy(
+                out_ref.at[spot],
+                rows_in.at[pl.ds(place * row_count, row_count)],
+                load_sem.at[place],
+            )
+            load.start()
+            loads.append(load)
+        for load in loads:
+            load.wait()
+        for expert in range(expert_count):
+            total[...] = jnp.zeros_like(total)
+
+            @pl.loop(0, depth // step_depth)
+            def _(step):
+                span = pl.ds(pl.multiple_of(step * step_depth, step_depth), step_depth)
+                total[...] += jnp.dot(
+                    rows_in[:, span],
+                    weights[expert, span, :],
+                    preferred_element_type=jnp.float32,
+                )
+
+            for place, spot in enumerate(spots):
+                up = total[place * row_count : (place + 1) * row_count, :]
+                share = share_ref[spot][:, expert : expert + 1]
+                hidden = up / (1.0 + jnp.exp(-up)) * share
+                hidden_ref[spot, :, pl.ds(expert * hidden_width, hidden_width)] = hidden.astype(
+                    hidden_ref.dtype
+                )
 
     def spread_diagonal(k):
         there = out_ref.at[block(-k, 1, 1, 0)]
@@ -84,6 +142,9 @@
         send(("t", k), src, spot, twin)
         if turn:
             spread_diagonal(order[turn - 1])
+            compute(order[turn - 1], 0)
+        else:
+            weight_copy.start()
         from_y = out_ref.at[block(-k, 1, 0, 0)]
         from_x = out_ref.at[block(-k, 0, 1, 0)]
         copies["y", k].wait_recv()
@@ -92,29 +153,47 @@
         send(("db", k), from_x.at[:, right], from_x.at[:, right], y_peer)
         send(("ty", k), from_y, from_y, twin)
         send(("tx", k), from_x, from_x, twin)
+        if turn:
+            compute(order[turn - 1], 1)
+    compute(order[-1], 0)
     spread_diagonal(order[-1])
-    for name, copy in copies.items():
+    compute(order[-1], 1)
+    for copy in copies.values():
         copy.wait_send()
-        if name[0] in ("t", "ty", "tx", "ta", "tb"):
-            copy.wait_recv()
-    keep.wait()
-
-
-def gather_rows(rows, block_total):
+
+
+def gather_up(rows, shares, up_weight):
+    block_total = shares.shape[0]
     row_count, width = rows.shape
-    return pl.pallas_call(
-        gather_kernel,
-        out_shape=jax.ShapeDtypeStruct((block_total, row_count, width), rows.dtype),
-        in_specs=[pl.BlockSpec(memory_space=pl.ANY)],
-        out_specs=pl.BlockSpec(memory_space=pl.ANY),
+    expert_count, _, hidden_width = up_weight.shape
+    _, hidden = pl.pallas_call(
+        gather_up_kernel,
+        out_shape=[
+            jax.ShapeDtypeStruct((block_total, row_count, width), rows.dtype),
+            jax.ShapeDtypeStruct((block_total, row_count, expert_count * hidden_width), rows.dtype),
+        ],
+        in_specs=[
+            pl.BlockSpec(memory_space=pl.ANY),
+            pl.BlockSpec(memory_space=pltpu.VMEM),
+            pl.BlockSpec(memory_space=pl.ANY),
+        ],
+        out_specs=[pl.BlockSpec(memory_space=pl.ANY), pl.BlockSpec(memory_space=pltpu.VMEM)],
         scratch_shapes=[
+            pltpu.VMEM(up_weight.shape, up_weight.dtype),
+            pltpu.VMEM((4 * row_count, width), rows.dtype),
+            pltpu.VMEM((4 * row_count, hidden_width), jnp.float32),
             pltpu.SemaphoreType.DMA((39,)),
             pltpu.SemaphoreType.DMA((39,)),
             pltpu.SemaphoreType.DMA,
+            pltpu.SemaphoreType.DMA((4,)),
+            pltpu.SemaphoreType.DMA,
         ],
-        compiler_params=pltpu.CompilerParams(collective_id=0, has_side_effects=True),
-        name="gather_rows",
-    )(rows)
+        compiler_params=pltpu.CompilerParams(
+            collective_id=0, has_side_effects=True, vmem_limit_bytes=56 * 1024 * 1024
+        ),
+        name="gather_up",
+    )(rows, shares, up_weight)
+    return hidden
 
 
 def reduce_kernel(part_ref, out_ref, mine, twin_in, diag_in, y_in, x_in, z_in, send_sem, recv_sem, load_sem):
@@ -235,52 +314,22 @@
     )(parts)
 
 
-def experts_by_kernels(norm_rows, routes, route_weight, up_weight, down_weight, capacity):
+def experts_by_kernels(norm_rows, routes, route_weight, up_weight, down_weight):
     row_count, model_dim = norm_rows.shape
-    seq_count, exp_count = lax.axis_size("seq"), lax.axis_size("exp")
-    block_total = seq_count * exp_count
-    local_experts = up_weight.shape[0]
+    local_experts, hidden_width, _ = down_weight.shape
     sheet = jnp.concatenate([routes.astype(jnp.float32), route_weight], axis=1).T
     sheets = lax.all_gather(sheet, ("seq", "exp"), axis=0, tiled=False)
     first = lax.axis_index("exp") * local_experts
-    local_ids = (first + jnp.arange(local_experts)).astype(jnp.float32)[:, None, None, None]
-    hits = sheets[None, :, :2] == local_ids
-    member = jnp.any(hits, axis=2)
-    member_weight = jnp.sum(jnp.where(hits, sheets[None, :, 2:], 0.0), axis=2)
-    earlier = jnp.triu(jnp.ones((row_count, row_count), jnp.bfloat16), 1)
-    rank = jnp.einsum(
-        "lbt,tu->lbu",
-        member.astype(jnp.bfloat16),
-        earlier,
+    local_ids = (first + jnp.arange(local_experts)).astype(jnp.float32)
+    hits = sheets[:, :2, :, None] == local_ids
+    shares = jnp.sum(jnp.where(hits, sheets[:, 2:, :, None], 0.0), axis=1)
+    hidden = gather_up(norm_rows, shares, up_weight)
+    spread = jnp.dot(
+        hidden.reshape(-1, local_experts * hidden_width),
+        down_weight.reshape(local_experts * hidden_width, model_dim),
         preferred_element_type=jnp.float32,
-    ).astype(jnp.int32)
-    slot = rank + (jnp.arange(block_total, dtype=jnp.int32) % exp_count)[None, :, None] * capacity
-    grouped = (local_experts, seq_count, 1, exp_count * row_count)
-    slots = exp_count * capacity
-    pick = (jnp.arange(slots, dtype=jnp.int32)[:, None] == slot.reshape(grouped)) & member.reshape(
-        grouped
-    )
-    slot_weight = jnp.sum(jnp.where(pick, member_weight.reshape(grouped), 0.0), axis=3)
-    pick = pick.astype(jnp.bfloat16)
-    rows = gather_rows(norm_rows, block_total)
-    rows = rows.reshape(seq_count, exp_count * row_count, model_dim)
-    parts = []
-    for expert in range(local_experts):
-        packed = jnp.einsum(
-            "gst,gtd->gsd", pick[expert], rows, preferred_element_type=jnp.float32
-        ).astype(jnp.bfloat16)
-        packed = packed.reshape(seq_count * slots, model_dim)
-        hidden = jax.nn.silu(
-            jnp.dot(packed, up_weight[expert], preferred_element_type=jnp.float32)
-        ).astype(jnp.bfloat16)
-        part = jnp.dot(hidden, down_weight[expert], preferred_element_type=jnp.float32)
-        part = (part * slot_weight[expert].reshape(-1, 1)).astype(jnp.bfloat16)
-        parts.append(part.reshape(seq_count, slots, model_dim))
-    spread = sum(
-        jnp.einsum("gst,gsd->gtd", pick[expert], parts[expert], preferred_element_type=jnp.float32)
-        for expert in range(local_experts)
     ).astype(jnp.bfloat16)
-    return reduce_rows(spread.reshape(block_total, row_count, model_dim))
+    return reduce_rows(spread.reshape(-1, row_count, model_dim))
 
 
 def expert_part(rows, up_weight, down_weight):
@@ -370,9 +419,7 @@
     norm_rows = (token_float * lax.rsqrt(row_square + 1e-06) * moe_gain).astype(jnp.bfloat16)
     capacity = row_count * 10 // (4 * EXPERTS)
     if (lax.axis_size("seq"), lax.axis_size("exp")) == (2 * Z_LEN, 4):
-        combined = experts_by_kernels(
-            norm_rows, routes, route_weight, up_weight, down_weight, capacity
-        )
+        combined = experts_by_kernels(norm_rows, routes, route_weight, up_weight, down_weight)
         return (token_float + combined).astype(jnp.bfloat16)
     flat_ids = routes.reshape(-1)
     onehot = (flat_ids[:, None] == jnp.arange(EXPERTS, dtype=jnp.int32)[None, :]).astype(jnp.int32)

time: 494 us -> 495 us (level); the launches traced: 488 us -> 495 us
  matrix products: 152 us -> 72.7 us
  Pallas kernels: 223 us -> 279 us
  waiting for transfers between devices: 32.2 us -> 65.7 us
    dot_general x9 -> x1, matrix products: 146 us -> 66.9 us  [experts_by_kernels(): jnp.dot(hidden.reshape(-1, local_experts * hidden_width), down_weight.res...]
    pallas_call x1, Pallas kernels: 112 us -> 166 us  [gather_up(): pl.pallas_call(gather_up_kernel, out_shape=[jax.ShapeDtypeStruct((block_t...]
    all_gather x1, waiting for transfers between devices: 21.4 us -> 65.7 us  [per_device(): lax.all_gather(payload, 'seq', axis=0, tiled=False).astype(jnp.float32)]
    all_to_all x1, waiting for transfers between devices: 10.8 us -> 0.01 us  [per_device(): lax.all_to_all(mixed_rows, 'exp', split_axis=0, concat_axis=1, tiled=True)]
  transfers between devices with their start and end apart: 2 -> 2, of which waited for: 2 -> 1; matrix products, arithmetic and copies ran while one was open for 0% -> 0% of each run, Pallas kernels for 0% -> 0%
where the time goes in v3:
time: 495 us
  Pallas kernels  279 us (56%)
  matrix products  72.7 us (15%)
  waiting for transfers between devices  65.7 us (13%)
  blocking collectives  41.9 us (8%)
  between operations  13.7 us (3%)
  other arithmetic  13 us (3%)
  local copies, waits for them, and re-layouts  5.01 us (1%)
    pallas_call x1, Pallas kernels, gather_up(): pl.pallas_call(gather_up_kernel, out_shape=[jax.ShapeDtypeStruct((block_t...  166 us
    pallas_call x1, Pallas kernels, reduce_rows(): pl.pallas_call(reduce_kernel, out_shape=jax.ShapeDtypeStruct((row_count,...  113 us
    dot_general x1, matrix products, experts_by_kernels(): jnp.dot(hidden.reshape(-1, local_experts * hidden_width), down_weight.res...  66.9 us
    all_gather x1, waiting for transfers between devices, per_device(): lax.all_gather(payload, 'seq', axis=0, tiled=False).astype(jnp.float32)  65.7 us
    all_gather x1, blocking collectives, experts_by_kernels(): sheets = lax.all_gather(sheet, ('seq', 'exp'), axis=0, tiled=False)  41.9 us
  transfers between devices with their start and end apart: 2, of which 1 were waited for; matrix products, arithmetic and copies ran while one was open for 0% of the time, Pallas kernels for 0%

profile of v3, /device:TPU:0, one launch (start us, length us, event | category | flops | bytes accessed | tf_op | source)
XLA Modules:
  0.0 494.6 jit_solution(9913004201777681894)
XLA Ops:
  6.5 0.0 copy-start
  6.5 0.0 copy-start.1
  6.5 0.0 all-gather.5.cloned.1.call-start
  6.5 0.8 reshape.230
  7.4 0.6 reduce-window.6
  8.0 0.2 slice_reduce_fusion
  8.1 0.1 copy.69
  8.4 0.1 copy.70
  8.5 0.0 copy-done
  8.5 0.3 copy.71
  8.8 0.0 copy-done.1
  8.8 0.3 copy.72
  9.1 0.0 copy-start.3
  9.1 0.0 copy-start.2
  9.1 0.4 fusion.6
  9.5 0.8 fusion.10
  10.3 0.0 all-gather.5.cloned.1.call-update
  10.4 0.1 copy.98
  10.4 0.0 copy-done.3
  10.4 0.1 copy.74
  10.5 0.1 copy-done.2
  10.6 0.3 copy.75
  11.0 65.7 %all-gather.5.cloned.1.call-done = bf16[104,128,128]{2,1,0:T(8,128)(2,1)} async-done(((bf16[13,128,128]{2,1,0:T(8,128)(2,1)}), bf16[104,128,128]{2,1,0:T(8,128)(2,1)}) %all-gather.5.cloned.1.call-update) | async-done | bytes 3407888 | tf_op jit(solution)/shard_map/all_gather | solution.py:390
  76.7 0.7 slice_convert_fusion
  77.4 0.1 select_reduce_fusion.1
  77.5 0.1 select_bitcast_fusion
  77.6 2.6 multiply_reduce_fusion
  80.2 1.6 fusion.3
  81.9 0.0 copy-start.5
  81.9 3.8 fusion.1
  85.7 0.0 copy-done.5
  85.7 1.7 fusion.2
  87.4 0.5 copy.81
  87.8 2.2 add_convert_fusion.1
  90.0 0.0 copy-start.6
  90.0 0.0 copy-start.7
  90.0 3.6 all-to-all-start
  93.7 0.0 copy-done.6
  93.7 0.0 copy-done.7
  93.7 41.9 %all-gather.2 = f32[32,4,64]{2,1,0:T(4,128)S(1)} all-gather(f32[1,4,64]{2,1,0:T(4,128)S(1)} %maximum_bitcast_fusion), channel_id=3, replica_groups=mesh['seq'=8,'exp'=4] {'seq','exp'}, dimensions={0}, use_global_device_ids=true | all-gather | bytes 33792 | tf_op jit(solution)/shard_map/all_gather | solution.py:321
  135.7 0.1 select_reduce_fusion
  135.8 1.4 copy.85.share_ref
  137.2 0.0 all-to-all-done
  137.2 0.3 fusion
  137.5 0.2 convert_bitcast_fusion
  137.6 0.0 copy-start.4
  137.7 0.1 copy.100
  137.8 0.6 copy-done.4
  138.4 1.1 multiply_convert_fusion.1.own_ref
  139.5 166.4 %gather_up.1 = (bf16[32,64,6144]{2,1,0:T(8,128)(2,1)}, bf16[32,64,2304]{2,1,0:T(8,128)(2,1)}) custom-call(bf16[64,6144]{1,0:T(8,128)(2,1)} %multiply_convert_fusion.1.own_ref, f32[32,64,2]{2,1,0:T(8,128)} %copy.85.share_ref, bf16[2,6144,1152]{2,1,0:T(8,128)(2,1)} %weight_ref.1), custom_call_target="tpu_custom_call" | custom-call | tf_op jit(solution)/shard_map/gather_up/pallas_call | solution.py:169
  305.9 66.9 %convolution_convert_fusion = bf16[2048,6144]{1,0:T(8,128)(2,1)} fusion(bf16[2048,2304]{1,0:T(8,128)(2,1)} %bitcast.98, bf16[2304,6144]{1,0:T(8,128)(2,1)} %bitcast.97), kind=kOutput, calls=%fused_computation | convolution fusion | flops 57994641408 | bytes 62914560 | tf_op jit(solution)/shard_map/dot_general | solution.py:327
  372.8 112.5 %reduce_rows.1 = f32[64,6144]{1,0:T(8,128)} custom-call(bf16[32,64,6144]{2,1,0:T(8,128)(2,1)} %bitcast.73), custom_call_target="tpu_custom_call" | custom-call | tf_op jit(solution)/shard_map/reduce_rows/pallas_call | solution.py:294
  485.3 2.4 add_convert_fusion
  (24 shorter events, 0.3 us)
Async XLA Ops:
  6.5 2.0 copy-start
  6.5 2.2 copy-start.1
  6.5 70.2 %all-gather.5.cloned.1.call-start = ((), (), s32[]{:S(2)}) async-start(), calls=%async_computation.1 | async-start | bytes 3833856 | tf_op jit(solution)/shard_map/all_gather | solution.py:390
  9.1 1.4 copy-start.3
  9.1 1.6 copy-start.2
  81.9 3.8 copy-start.5
  90.0 3.6 copy-start.6
  90.0 3.7 copy-start.7
  90.0 47.1 %all-to-all-start = ((bf16[4,64,1536]{2,1,0:T(8,128)(2,1)}), bf16[4,64,1536]{2,1,0:T(8,128)(2,1)S(1)}, u32[]{:S(2)}, u32[]{:S(2)}) async-start(bf16[4,64,1536]{2,1,0:T(8,128)(2,1)} %bitcast.23), calls=%async_computation | async-start | bytes 1572864 | tf_op jit(solution)/shard_map/all_to_all | solution.py:415
  137.6 0.7 copy-start.4
Sparse Core Ops, SparseCore 0:
  10.4 66.2 all-gather.4
